TPU v7x, 256 devices: a whole 4x4x8 slice. The times are simulated.
256 devices in a mesh: vox: 32 (over z, y), col: 8 (over x, core).
Axes of the slice: x: 4, y: 4, z: 8, core: 2. Of those that a mesh axis runs over, the one named last changes fastest.
Arguments:
- start_modes: float32 [128, 131072], P('col', 'vox'), may hold values from -48 to 48
- start_dirs: float32 [128, 131072], P('col', 'vox'), may hold values from -6 to 6
- coupling: float32 [13, 131072], P(None, ('vox', 'col')), may hold values from 0.05 to 1
- relax_class: int32 [131072], P(('vox', 'col')), may hold values from 0 to 3
- relaxivity: float32 [4], replicated, may hold values from 0.5 to 4
Outputs:
- modes: float32 [128, 131072], P('col', 'vox')
- ritz: float32 [128, 128], replicated
All inputs are finite; a program needn't handle non-finite values.
Results may differ from a plain program's by a relative error of at most 0.0003.
Values sent between devices are 32-bit elements; how exact they have to be, the bound alone decides.
A program may use at most 64 MiB of HBM per device.

v0:
```python
import math
import jax
import jax.numpy as jnp
from jax import lax
from jax.sharding import PartitionSpec as P

NX = 256
NZ = 2
HALF = 13
ITERS = 2
QSTEPS = 3
offsets = [
    (a, b, c) for a in (-1, 0, 1) for b in (-1, 0, 1) for c in (-1, 0, 1) if (a, b, c) > (0, 0, 0)
]


def from_behind(block, axis, distance):
    devices = range(lax.axis_size(axis))
    route = [(i - distance, i) for i in devices if i - distance in devices]
    return lax.ppermute(block, axis, route)


def extended_2(block, sides, width):
    for axis, dim in sides:
        count = lax.axis_size(axis)
        forward = [(i, i + 1) for i in range(count - 1)]
        backward = [(target, source) for source, target in forward]
        low = lax.ppermute(
            lax.slice_in_dim(block, block.shape[dim] - width, None, axis=dim), axis, forward
        )
        high = lax.ppermute(lax.slice_in_dim(block, 0, width, axis=dim), axis, backward)
        block = jnp.concatenate([low, block, high], axis=dim)
    return block


def matmul(left, right):
    return jnp.dot(left, right, precision=lax.Precision.HIGHEST, preferred_element_type=jnp.float32)


def lower_solve(lower, rhs):
    return lax.linalg.triangular_solve(lower, rhs, left_side=True, lower=True)


def upper_solve(lower, rhs):
    return lax.linalg.triangular_solve(lower, rhs, left_side=True, lower=True, transpose_a=True)


def symmetric(matrix):
    return 0.5 * (matrix + matrix.T)


def project_pencil(gram_a, gram_b, count):
    sym_a = symmetric(gram_a)
    scales = lax.rsqrt(jnp.diagonal(gram_b) + 1e-06)
    normed_b = scales[:, None] * gram_b * scales[None, :]
    normed_a = scales[:, None] * sym_a * scales[None, :]
    lower = jnp.linalg.cholesky(normed_b)
    half_way = lower_solve(lower, normed_a)
    reduced = lower_solve(lower, half_way.T)
    shift = 2.0 * jnp.max(jnp.sum(jnp.abs(reduced), axis=1))
    iterate = jnp.eye(gram_a.shape[0], count, dtype=jnp.float32)
    for sweep_index in range(QSTEPS):
        iterate = shift * iterate - matmul(reduced, iterate)
        factor = jnp.linalg.cholesky(matmul(iterate.T, iterate))
        iterate = lower_solve(factor, iterate.T).T
    return scales[:, None] * upper_solve(lower, iterate)


def neighbour_sum(padded, coupled):
    rows_y = padded.shape[1] - 2
    rows_z = padded.shape[2] - 2
    rows_x = padded.shape[3] - 2
    total = jnp.zeros((padded.shape[0], rows_y, rows_z, rows_x), jnp.float32)
    for which, (step_y, step_z, step_x) in enumerate(offsets):
        ahead = padded[
            :,
            1 + step_y : 1 + step_y + rows_y,
            1 + step_z : 1 + step_z + rows_z,
            1 + step_x : 1 + step_x + rows_x,
        ]
        behind = padded[
            :,
            1 - step_y : 1 - step_y + rows_y,
            1 - step_z : 1 - step_z + rows_z,
            1 - step_x : 1 - step_x + rows_x,
        ]
        here = coupled[which, 1 : 1 + rows_y, 1 : 1 + rows_z, 1 : 1 + rows_x]
        back = coupled[
            which,
            1 - step_y : 1 - step_y + rows_y,
            1 - step_z : 1 - step_z + rows_z,
            1 - step_x : 1 - step_x + rows_x,
        ]
        total = total + here[None] * ahead
        total = total + back[None] * behind
    return total


def pad_plane(array):
    return jnp.pad(array, ((0, 0), (0, 0), (1, 1), (1, 1)))


def quotient(modes, images):
    total = lax.psum(matmul(modes, images.T), ("vox", "col"))
    return symmetric(total)


def on_device(start_modes, start_dirs, coupling, relax_class, relaxivity):
    local_voxels = coupling.shape[1]
    match = relax_class[:, None] == jnp.arange(relaxivity.shape[0], dtype=jnp.int32)[None, :]
    voxel_rate = jnp.sum(jnp.where(match, relaxivity[None, :], jnp.float32(0.0)), axis=1)
    damping = 1.0 / (1.0 + voxel_rate)
    own_coupling = coupling.reshape(HALF, 1, NZ, NX)
    before = from_behind(own_coupling, ("vox", "col"), 1)
    coupled = pad_plane(
        jnp.concatenate([before, own_coupling, jnp.zeros_like(own_coupling)], axis=1)
    )
    position = lax.axis_index(("vox", "col"))
    device_count = lax.axis_size(("vox", "col"))
    plane = jnp.ones((1, 1, NZ, NX), jnp.float32)
    upper_flag = (position > 0).astype(jnp.float32)
    lower_flag = (position < device_count - 1).astype(jnp.float32)
    unity = pad_plane(jnp.concatenate([upper_flag * plane, plane, lower_flag * plane], axis=1))
    degree = neighbour_sum(unity, coupled).reshape(local_voxels)
    diagonal = degree + voxel_rate

    def operate(field):
        count = field.shape[0]
        shaped = field.reshape(count, 1, NZ, NX)
        extended = extended_2(shaped, ((("vox", "col"), 1),), 1)
        padded = pad_plane(extended)
        return diagonal[None, :] * field - neighbour_sum(padded, coupled).reshape(
            count, local_voxels
        )

    modes, dirs = (
        lax.all_to_all(start_modes, "col", split_axis=1, concat_axis=0, tiled=True),
        lax.all_to_all(start_dirs, "col", split_axis=1, concat_axis=0, tiled=True),
    )
    count = modes.shape[0]
    images = operate(modes)
    dir_images = operate(dirs)
    ritz = quotient(modes, images)
    for iteration in range(ITERS):
        resid = images - matmul(ritz, modes)
        search = resid * damping[None, :]
        search_images = operate(search)
        basis = jnp.concatenate([modes, search, dirs], axis=0)
        basis_images = jnp.concatenate([images, search_images, dir_images], axis=0)
        local_a = matmul(basis, basis_images.T)
        local_b = matmul(basis, basis.T)
        gram_a, gram_b = lax.psum((local_a, local_b), ("vox", "col"))
        coeffs = project_pencil(gram_a, gram_b, count)
        modes = matmul(coeffs.T, basis)
        images = matmul(coeffs.T, basis_images)
        dirs = matmul(coeffs[count:].T, basis[count:])
        dir_images = matmul(coeffs[count:].T, basis_images[count:])
        ritz = quotient(modes, images)
    total_voxels = device_count * local_voxels
    scaled = modes * math.sqrt(total_voxels)
    modes_out = lax.all_to_all(scaled, "col", split_axis=0, concat_axis=1, tiled=True)
    return (modes_out, ritz)


def solution(mesh):
    in_specs = (P("col", "vox"), P("col", "vox"), P(None, ("vox", "col")), P(("vox", "col")), P())
    out_specs = (P("col", "vox"), P())
    return jax.shard_map(
        on_device, mesh=mesh, in_specs=in_specs, out_specs=out_specs, check_vma=False
    )
```

profile of v0, /device:TPU:1, one launch (start us, length us, event | category | flops | bytes accessed | tf_op | source)
XLA Modules:
  0.0 1733.3 jit_solution(11976527018198322847)
XLA Ops:
  8.8 6.6 all-to-all-start
  16.2 3.5 collective-permute-start
  25.2 4.1 all-to-all-start.1
  31.4 3.6 collective-permute-start.1
  36.0 2.9 collective-permute-start.6
  38.9 2.6 collective-permute-start.5
  41.6 2.3 select_maximum_fusion.6
  43.9 4.5 multiply_subtract_fusion.3
  49.6 3.4 select_maximum_fusion.2
  53.1 245.1 %all-reduce.15.cloned.1.call-done = f32[128,128]{0,1:T(8,128)} async-done(((f32[128,128]{0,1:T(8,128)}), f32[128,128]{0,1:T(8,128)}) %all-reduce.15.cloned.1.call-update) | async-done | bytes 65552 | tf_op jit(solution)/shard_map/psum | solution.py:104
  303.3 3.9 collective-permute-start.3
  307.2 5.4 fusion.64
  317.3 4.4 fusion.89
  325.0 256.1 %all-reduce.23.cloned.1.call-done = (f32[384,384]{1,0:T(8,128)}, f32[384,384]{0,1:T(8,128)}) async-done(((f32[384,384]{1,0:T(8,128)}, f32[384,384]{0,1:T(8,128)}), (f32[384,384]{1,0:T(8,128)}, f32[384,384]{0,1:T(8,128)})) %all-reduce.23.cloned.1.call-update) | async-done | bytes 1179664 | tf_op jit(solution)/shard_map/psum | solution.py:152
  581.2 6.6 gather_fusion
  590.4 11.7 cholesky.310
  602.2 9.8 custom-call.40
  614.4 11.7 cholesky.329
  626.2 9.9 custom-call.41
  637.5 11.7 cholesky.348
  652.6 5.9 while.12
  658.5 29.7 %custom-call.47 = f32[3,128,128]{1,2,0:T(8,128)S(1)} custom-call(f32[3,128,128]{2,1,0:T(8,128)S(1)} %get-tuple-element.49), custom_call_target="InvertDiagBlocksLowerTriangular" | custom-call | tf_op jit(solution)/shard_map/triangular_solve/custom-call.8 | solution.py:45
  695.7 11.7 cholesky.361
  708.7 9.8 custom-call.44
  720.8 11.7 cholesky.372
  733.9 9.8 custom-call.45
  745.5 11.9 cholesky.383
  758.7 9.8 custom-call.46
  773.6 237.5 %all-reduce.17.cloned.1.call-done = f32[128,128]{1,0:T(8,128)} async-done(((f32[128,128]{1,0:T(8,128)}), f32[128,128]{1,0:T(8,128)}) %all-reduce.17.cloned.1.call-update) | async-done | bytes 65552 | tf_op jit(solution)/shard_map/psum | solution.py:104
  1015.4 3.6 collective-permute-start.7
  1024.6 4.4 fusion.39
  1031.5 259.7 %all-reduce.21.cloned.1.call-done = (f32[384,384]{1,0:T(8,128)}, f32[384,384]{0,1:T(8,128)}) async-done(((f32[384,384]{1,0:T(8,128)}, f32[384,384]{0,1:T(8,128)}), (f32[384,384]{1,0:T(8,128)}, f32[384,384]{0,1:T(8,128)})) %all-reduce.21.cloned.1.call-update) | async-done | bytes 1179664 | tf_op jit(solution)/shard_map/psum | solution.py:152
  1291.2 6.6 gather_fusion.1
  1300.6 11.7 cholesky.396
  1312.4 9.8 custom-call.48
  1324.5 11.7 cholesky.415
  1336.3 10.2 custom-call.49
  1347.8 11.7 cholesky.434
  1363.5 6.4 while.13
  1369.9 29.7 %custom-call.55 = f32[3,128,128]{1,2,0:T(8,128)S(1)} custom-call(f32[3,128,128]{2,1,0:T(8,128)S(1)} %get-tuple-element.52), custom_call_target="InvertDiagBlocksLowerTriangular" | custom-call | tf_op jit(solution)/shard_map/triangular_solve/custom-call.8 | solution.py:45
  1407.1 11.7 cholesky.447
  1420.1 9.8 custom-call.52
  1432.0 11.7 cholesky.458
  1445.0 9.8 custom-call.53
  1456.7 11.9 cholesky.469
  1470.0 9.8 custom-call.54
  1485.0 7.1 all-to-all-start.2
  1492.1 231.0 %all-reduce.19.cloned.1.call-done = f32[128,128]{1,0:T(8,128)} async-done(((f32[128,128]{1,0:T(8,128)}), f32[128,128]{1,0:T(8,128)}) %all-reduce.19.cloned.1.call-update) | async-done | bytes 65552 | tf_op jit(solution)/shard_map/psum | solution.py:104
  (329 shorter events, 108.3 us)
Async XLA Ops:
  8.8 16.4 all-to-all-start
  16.2 8.8 collective-permute-start
  25.2 10.6 all-to-all-start.1
  29.3 268.9 %all-reduce.15.cloned.1.call-start = ((), (), s32[]{:S(2)}) async-start(), calls=%async_computation.3 | async-start | bytes 131072 | tf_op jit(solution)/shard_map/psum | solution.py:104
  29.5 12.1 collective-permute-start.2
  31.4 10.1 collective-permute-start.1
  35.1 13.3 copy-start.21
  35.1 13.3 copy-start.23
  35.1 13.3 copy-start.25
  35.1 13.3 copy-start.27
  35.2 13.3 copy-start.29
  35.2 13.3 copy-start.31
  35.2 13.3 copy-start.33
  35.8 17.2 copy-start.35
  36.0 12.5 copy-start.15
  36.0 13.6 collective-permute-start.6
  38.9 10.7 collective-permute-start.5
  49.6 531.6 %all-reduce.23.cloned.1.call-start = ((), (), s32[]{:S(2)}) async-start(), calls=%async_computation.7 | async-start | bytes 2359296 | tf_op jit(solution)/shard_map/psum | solution.py:152
  301.3 13.6 copy-start.16
  301.3 13.6 collective-permute-start.4
  303.3 11.6 collective-permute-start.3
  312.6 4.6 copy-start.22
  312.6 4.6 copy-start.24
  312.6 4.6 copy-start.26
  312.6 4.6 copy-start.28
  325.0 686.1 %all-reduce.17.cloned.1.call-start = ((), (), s32[]{:S(2)}) async-start(), calls=%async_computation.4 | async-start | bytes 131072 | tf_op jit(solution)/shard_map/psum | solution.py:104
  581.2 6.6 copy-start.2
  581.2 7.7 copy-start
  590.4 11.7 copy-start.12
  744.1 26.5 %copy-start.7 = (f32[128,512]{1,0:T(8,128)S(1)}, f32[128,512]{1,0:T(8,128)}, u32[]{:S(2)}) copy-start(f32[128,512]{1,0:T(8,128)} %copy-done.6) | copy-start | bytes 786436
  744.1 26.5 %copy-start.9 = (f32[128,512]{1,0:T(8,128)S(1)}, f32[128,512]{1,0:T(8,128)}, u32[]{:S(2)}) copy-start(f32[128,512]{1,0:T(8,128)} %copy-done.8) | copy-start | bytes 786436
  770.2 241.8 %copy-start.37 = (f32[512]{0:T(512)S(1)}, f32[512]{0:T(512)}, u32[]{:S(2)}) copy-start(f32[512]{0:T(512)} %get-tuple-element.163) | copy-start | bytes 6148
  771.3 257.8 %copy-start.4 = (f32[128,512]{1,0:T(8,128)}, f32[128,512]{1,0:T(8,128)S(1)}, u32[]{:S(2)}) copy-start(f32[128,512]{1,0:T(8,128)S(1)} %fusion.13) | copy-start | bytes 786436
  773.1 518.2 %all-reduce.21.cloned.1.call-start = ((), (), s32[]{:S(2)}) async-start(), calls=%async_computation.6 | async-start | bytes 2359296 | tf_op jit(solution)/shard_map/psum | solution.py:152
  773.6 255.6 %copy-start.10 = (f32[128,512]{1,0:T(8,128)}, f32[128,512]{1,0:T(8,128)S(1)}, u32[]{:S(2)}) copy-start(f32[128,512]{1,0:T(8,128)S(1)} %fusion.15) | copy-start | bytes 786436
  1013.5 8.3 collective-permute-start.8
  1015.4 6.9 collective-permute-start.7
  1019.5 9.7 copy-start.17
  1029.2 268.7 %copy-start.19 = (f32[128,512]{1,0:T(8,128)}, f32[128,512]{1,0:T(8,128)S(1)}, u32[]{:S(2)}) copy-start(f32[128,512]{1,0:T(8,128)S(1)} %multiply_subtract_fusion) | copy-start | bytes 786436
  1031.5 691.6 %all-reduce.19.cloned.1.call-start = ((), (), s32[]{:S(2)}) async-start(), calls=%async_computation.5 | async-start | bytes 131072 | tf_op jit(solution)/shard_map/psum | solution.py:104
  1291.2 6.7 copy-start.3
  1291.2 7.7 copy-start.1
  1300.5 11.7 copy-start.13
  1454.8 26.9 %copy-start.11 = (f32[128,512]{1,0:T(8,128)S(1)}, f32[128,512]{1,0:T(8,128)}, u32[]{:S(2)}) copy-start(f32[128,512]{1,0:T(8,128)} %copy-done.10) | copy-start | bytes 786436
  1455.9 27.2 %copy-start.5 = (f32[128,512]{1,0:T(8,128)S(1)}, f32[128,512]{1,0:T(8,128)}, u32[]{:S(2)}) copy-start(f32[128,512]{1,0:T(8,128)} %copy-done.4) | copy-start | bytes 786436
  1455.9 27.2 %copy-start.18 = (f32[128,512]{1,0:T(8,128)S(1)}, f32[128,512]{1,0:T(8,128)}, u32[]{:S(2)}) copy-start(f32[128,512]{1,0:T(8,128)} %copy-done.17) | copy-start | bytes 786436
  1455.9 27.2 %copy-start.20 = (f32[128,512]{1,0:T(8,128)S(1)}, f32[128,512]{1,0:T(8,128)}, u32[]{:S(2)}) copy-start(f32[128,512]{1,0:T(8,128)} %copy-done.19) | copy-start | bytes 786436
  1485.0 240.7 %all-to-all-start.2 = ((f32[8,16,512]{2,1,0:T(8,128)}), f32[8,16,512]{2,1,0:T(8,128)S(1)}, u32[]{:S(2)}, u32[]{:S(2)}) async-start(f32[8,16,512]{2,1,0:T(8,128)} %bitcast.87), calls=%async_computation.2 | async-start | bytes 524288 | tf_op jit(solution)/shard_map/all_to_all | solution.py:161
  (7 other events, 23.2 us)
Sparse Core Ops, SparseCore 0:
  49.7 248.4 all-reduce.14
  325.1 256.0 all-reduce.22
  773.2 237.8 all-reduce.16
  1031.6 259.5 all-reduce.20
  1485.1 237.9 all-reduce.18
where the time goes:
time: 1740 us; the launch traced here: 1730 us
  waiting for transfers between devices  1230 us (71%)
  other arithmetic  348 us (20%)
  matrix products  48.7 us (3%)
  starting transfers between devices  44.1 us (3%)
  local copies, waits for them, and re-layouts  41.4 us (2%)
  between operations  21 us (1%)
    psum x3, waiting for transfers between devices, quotient(): total = lax.psum(matmul(modes, images.T), ('vox', 'col'))  714 us
    psum x2, waiting for transfers between devices, on_device(): gram_a, gram_b = lax.psum((local_a, local_b), ('vox', 'col'))  516 us
    another operation x21, other arithmetic, project_pencil(): lower = jnp.linalg.cholesky(normed_b)  114 us
    another operation x18, other arithmetic, project_pencil(): factor = jnp.linalg.cholesky(matmul(iterate.T, iterate))  74.7 us
    another operation x12, other arithmetic, lower_solve(): return lax.linalg.triangular_solve(lower, rhs, left_side=True, lower=True)  62.8 us
    another operation x5, other arithmetic, upper_solve(): lax.linalg.triangular_solve(lower, rhs, left_side=True, lower=True, trans...  59.5 us
  transfers between devices with their start and end apart: 17, of which 6 were waited for; matrix products, arithmetic and copies ran while one was open for 2% of the time, Pallas kernels for 0%

commit v1 on v0

--- a/solution.py
+++ b/solution.py
@@ -149,7 +149,7 @@
         basis_images = jnp.concatenate([images, search_images, dir_images], axis=0)
         local_a = matmul(basis, basis_images.T)
         local_b = matmul(basis, basis.T)
-        gram_a, gram_b = lax.psum((local_a, local_b), ("vox", "col"))
+        gram_a, gram_b = lax.psum(lax.psum((local_a, local_b), "col"), "vox")
         coeffs = project_pencil(gram_a, gram_b, count)
         modes = matmul(coeffs.T, basis)
         images = matmul(coeffs.T, basis_images)

time: 1740 us -> 1660 us (0.954)
  waiting for transfers between devices: 1230 us -> 1150 us
    psum x2 -> x4, waiting for transfers between devices: 516 us -> 434 us  [on_device(): gram_a, gram_b = lax.psum(lax.psum((local_a, local_b), 'col'), 'vox')]
  transfers between devices with their start and end apart: 17 -> 19, of which waited for: 6 -> 8; matrix products, arithmetic and copies ran while one was open for 2% -> 2% of each run, Pallas kernels for 0% -> 0%
where the time goes in v1:
time: 1660 us
  waiting for transfers between devices  1150 us (69%)
  other arithmetic  348 us (21%)
  matrix products  48.7 us (3%)
  starting transfers between devices  46.6 us (3%)
  local copies, waits for them, and re-layouts  41.7 us (3%)
  between operations  21.3 us (1%)
    psum x3, waiting for transfers between devices, quotient(): total = lax.psum(matmul(modes, images.T), ('vox', 'col'))  715 us
    psum x4, waiting for transfers between devices, on_device(): gram_a, gram_b = lax.psum(lax.psum((local_a, local_b), 'col'), 'vox')  434 us
    another operation x21, other arithmetic, project_pencil(): lower = jnp.linalg.cholesky(normed_b)  114 us
    another operation x18, other arithmetic, project_pencil(): factor = jnp.linalg.cholesky(matmul(iterate.T, iterate))  74.7 us
    another operation x12, other arithmetic, lower_solve(): return lax.linalg.triangular_solve(lower, rhs, left_side=True, lower=True)  62.8 us
    another operation x5, other arithmetic, upper_solve(): lax.linalg.triangular_solve(lower, rhs, left_side=True, lower=True, trans...  59.5 us
  transfers between devices with their start and end apart: 19, of which 8 were waited for; matrix products, arithmetic and copies ran while one was open for 2% of the time, Pallas kernels for 0%

profile of v1, /device:TPU:1, one launch (start us, length us, event | category | flops | bytes accessed | tf_op | source)
XLA Modules:
  0.0 1656.5 jit_solution(1726911456861507876)
XLA Ops:
  8.8 6.6 all-to-all-start
  16.2 3.5 collective-permute-start
  25.2 4.1 all-to-all-start.1
  31.4 3.6 collective-permute-start.1
  36.0 2.9 collective-permute-start.6
  43.9 4.5 multiply_subtract_fusion.3
  49.6 3.4 select_maximum_fusion.2
  53.1 245.1 %all-reduce.19.cloned.1.call-done = f32[128,128]{0,1:T(8,128)} async-done(((f32[128,128]{0,1:T(8,128)}), f32[128,128]{0,1:T(8,128)}) %all-reduce.19.cloned.1.call-update) | async-done | bytes 65552 | tf_op jit(solution)/shard_map/psum | solution.py:104
  303.3 3.9 collective-permute-start.3
  307.1 5.4 fusion.64
  317.3 4.4 fusion.89
  325.0 65.6 %all-reduce.31.cloned.1.call-done = (f32[384,384]{1,0:T(8,128)}, f32[384,384]{0,1:T(8,128)}) async-done(((f32[384,384]{1,0:T(8,128)}, f32[384,384]{0,1:T(8,128)}), (f32[384,384]{1,0:T(8,128)}, f32[384,384]{0,1:T(8,128)})) %all-reduce.31.cloned.1.call-update) | async-done | bytes 1179664 | tf_op jit(solution)/shard_map/psum | solution.py:152
  390.7 150.0 %all-reduce.27.cloned.1.call-done = (f32[384,384]{1,0:T(8,128)}, f32[384,384]{0,1:T(8,128)}) async-done(((f32[384,384]{1,0:T(8,128)}, f32[384,384]{0,1:T(8,128)}), (f32[384,384]{1,0:T(8,128)}, f32[384,384]{0,1:T(8,128)})) %all-reduce.27.cloned.1.call-update) | async-done | bytes 1179664 | tf_op jit(solution)/shard_map/psum | solution.py:152
  540.7 6.8 gather_fusion
  550.2 11.7 cholesky.310
  562.0 9.8 custom-call.40
  574.2 11.7 cholesky.329
  585.9 9.9 custom-call.41
  597.2 11.7 cholesky.348
  612.3 5.9 while.12
  618.2 29.7 %custom-call.47 = f32[3,128,128]{1,2,0:T(8,128)S(1)} custom-call(f32[3,128,128]{2,1,0:T(8,128)S(1)} %get-tuple-element.49), custom_call_target="InvertDiagBlocksLowerTriangular" | custom-call | tf_op jit(solution)/shard_map/triangular_solve/custom-call.8 | solution.py:45
  655.4 11.7 cholesky.361
  668.5 9.8 custom-call.44
  680.6 11.7 cholesky.372
  693.6 9.8 custom-call.45
  705.3 11.9 cholesky.383
  718.5 9.8 custom-call.46
  733.3 239.5 %all-reduce.21.cloned.1.call-done = f32[128,128]{1,0:T(8,128)} async-done(((f32[128,128]{1,0:T(8,128)}), f32[128,128]{1,0:T(8,128)}) %all-reduce.21.cloned.1.call-update) | async-done | bytes 65552 | tf_op jit(solution)/shard_map/psum | solution.py:104
  977.2 3.6 collective-permute-start.7
  986.4 4.4 fusion.39
  993.3 69.0 %all-reduce.29.cloned.1.call-done = (f32[384,384]{1,0:T(8,128)}, f32[384,384]{0,1:T(8,128)}) async-done(((f32[384,384]{1,0:T(8,128)}, f32[384,384]{0,1:T(8,128)}), (f32[384,384]{1,0:T(8,128)}, f32[384,384]{0,1:T(8,128)})) %all-reduce.29.cloned.1.call-update) | async-done | bytes 1179664 | tf_op jit(solution)/shard_map/psum | solution.py:152
  1062.4 149.9 %all-reduce.25.cloned.1.call-done = (f32[384,384]{1,0:T(8,128)}, f32[384,384]{0,1:T(8,128)}) async-done(((f32[384,384]{1,0:T(8,128)}, f32[384,384]{0,1:T(8,128)}), (f32[384,384]{1,0:T(8,128)}, f32[384,384]{0,1:T(8,128)})) %all-reduce.25.cloned.1.call-update) | async-done | bytes 1179664 | tf_op jit(solution)/shard_map/psum | solution.py:152
  1212.2 6.7 gather_fusion.1
  1221.6 11.7 cholesky.396
  1233.4 9.8 custom-call.48
  1245.6 11.7 cholesky.415
  1257.3 10.2 custom-call.49
  1268.8 11.7 cholesky.434
  1284.5 6.4 while.13
  1290.9 29.7 %custom-call.55 = f32[3,128,128]{1,2,0:T(8,128)S(1)} custom-call(f32[3,128,128]{2,1,0:T(8,128)S(1)} %get-tuple-element.52), custom_call_target="InvertDiagBlocksLowerTriangular" | custom-call | tf_op jit(solution)/shard_map/triangular_solve/custom-call.8 | solution.py:45
  1328.1 11.7 cholesky.447
  1341.1 9.8 custom-call.52
  1353.0 11.7 cholesky.458
  1366.0 9.8 custom-call.53
  1377.7 11.9 cholesky.469
  1391.0 9.8 custom-call.54
  1406.0 9.6 all-to-all-start.2
  1415.6 230.5 %all-reduce.23.cloned.1.call-done = f32[128,128]{1,0:T(8,128)} async-done(((f32[128,128]{1,0:T(8,128)}), f32[128,128]{1,0:T(8,128)}) %all-reduce.23.cloned.1.call-update) | async-done | bytes 65552 | tf_op jit(solution)/shard_map/psum | solution.py:104
  (335 shorter events, 113.3 us)
Async XLA Ops:
  8.8 16.4 all-to-all-start
  16.2 8.8 collective-permute-start
  25.2 10.6 all-to-all-start.1
  29.3 268.9 %all-reduce.19.cloned.1.call-start = ((), (), s32[]{:S(2)}) async-start(), calls=%async_computation.3 | async-start | bytes 131072 | tf_op jit(solution)/shard_map/psum | solution.py:104
  29.5 12.1 collective-permute-start.2
  31.4 10.1 collective-permute-start.1
  35.1 13.3 copy-start.21
  35.1 13.3 copy-start.23
  35.1 13.3 copy-start.25
  35.1 13.3 copy-start.27
  35.2 13.3 copy-start.29
  35.2 13.3 copy-start.31
  35.2 13.3 copy-start.33
  35.8 17.2 %copy-start.35 = (f32[512]{0:T(512)}, f32[512]{0:T(512)S(1)}, u32[]{:S(2)}) copy-start(f32[512]{0:T(512)S(1)} %get-tuple-element.168) | copy-start | bytes 6148
  36.0 12.5 copy-start.15
  36.0 13.6 collective-permute-start.6
  38.9 10.7 collective-permute-start.5
  49.5 341.0 %all-reduce.31.cloned.1.call-start = ((), (), s32[]{:S(2)}) async-start(), calls=%async_computation.9 | async-start | bytes 2359296 | tf_op jit(solution)/shard_map/psum | solution.py:152
  301.2 13.6 copy-start.16
  301.2 13.6 collective-permute-start.4
  303.3 11.6 collective-permute-start.3
  312.6 4.6 copy-start.22
  312.6 4.6 copy-start.24
  324.9 215.8 %all-reduce.27.cloned.1.call-start = ((), (), s32[]{:S(2)}) async-start(), calls=%async_computation.7 | async-start | bytes 2359296 | tf_op jit(solution)/shard_map/psum | solution.py:152
  390.6 582.3 %all-reduce.21.cloned.1.call-start = ((), (), s32[]{:S(2)}) async-start(), calls=%async_computation.4 | async-start | bytes 131072 | tf_op jit(solution)/shard_map/psum | solution.py:104
  540.7 6.8 copy-start.2
  540.7 7.9 copy-start
  550.1 11.7 copy-start.12
  703.8 26.5 %copy-start.7 = (f32[128,512]{1,0:T(8,128)S(1)}, f32[128,512]{1,0:T(8,128)}, u32[]{:S(2)}) copy-start(f32[128,512]{1,0:T(8,128)} %copy-done.6) | copy-start | bytes 786436
  703.9 26.5 %copy-start.9 = (f32[128,512]{1,0:T(8,128)S(1)}, f32[128,512]{1,0:T(8,128)}, u32[]{:S(2)}) copy-start(f32[128,512]{1,0:T(8,128)} %copy-done.8) | copy-start | bytes 786436
  729.9 243.8 %copy-start.37 = (f32[512]{0:T(512)S(1)}, f32[512]{0:T(512)}, u32[]{:S(2)}) copy-start(f32[512]{0:T(512)} %get-tuple-element.167) | copy-start | bytes 6148
  731.0 259.9 %copy-start.4 = (f32[128,512]{1,0:T(8,128)}, f32[128,512]{1,0:T(8,128)S(1)}, u32[]{:S(2)}) copy-start(f32[128,512]{1,0:T(8,128)S(1)} %fusion.13) | copy-start | bytes 786436
  732.8 329.5 %all-reduce.29.cloned.1.call-start = ((), (), s32[]{:S(2)}) async-start(), calls=%async_computation.8 | async-start | bytes 2359296 | tf_op jit(solution)/shard_map/psum | solution.py:152
  733.3 257.6 %copy-start.10 = (f32[128,512]{1,0:T(8,128)}, f32[128,512]{1,0:T(8,128)S(1)}, u32[]{:S(2)}) copy-start(f32[128,512]{1,0:T(8,128)S(1)} %fusion.15) | copy-start | bytes 786436
  975.2 8.3 collective-permute-start.8
  977.2 6.9 collective-permute-start.7
  981.3 9.6 copy-start.17
  990.9 228.0 %copy-start.19 = (f32[128,512]{1,0:T(8,128)}, f32[128,512]{1,0:T(8,128)S(1)}, u32[]{:S(2)}) copy-start(f32[128,512]{1,0:T(8,128)S(1)} %multiply_subtract_fusion) | copy-start | bytes 786436
  993.2 219.0 %all-reduce.25.cloned.1.call-start = ((), (), s32[]{:S(2)}) async-start(), calls=%async_computation.6 | async-start | bytes 2359296 | tf_op jit(solution)/shard_map/psum | solution.py:152
  1062.3 583.7 %all-reduce.23.cloned.1.call-start = ((), (), s32[]{:S(2)}) async-start(), calls=%async_computation.5 | async-start | bytes 131072 | tf_op jit(solution)/shard_map/psum | solution.py:104
  1212.2 6.7 copy-start.3
  1212.2 7.8 copy-start.1
  1221.6 11.7 copy-start.13
  1375.9 26.9 %copy-start.11 = (f32[128,512]{1,0:T(8,128)S(1)}, f32[128,512]{1,0:T(8,128)}, u32[]{:S(2)}) copy-start(f32[128,512]{1,0:T(8,128)} %copy-done.10) | copy-start | bytes 786436
  1376.9 27.3 %copy-start.5 = (f32[128,512]{1,0:T(8,128)S(1)}, f32[128,512]{1,0:T(8,128)}, u32[]{:S(2)}) copy-start(f32[128,512]{1,0:T(8,128)} %copy-done.4) | copy-start | bytes 786436
  1376.9 27.2 %copy-start.18 = (f32[128,512]{1,0:T(8,128)S(1)}, f32[128,512]{1,0:T(8,128)}, u32[]{:S(2)}) copy-start(f32[128,512]{1,0:T(8,128)} %copy-done.17) | copy-start | bytes 786436
  1377.0 27.2 %copy-start.20 = (f32[128,512]{1,0:T(8,128)S(1)}, f32[128,512]{1,0:T(8,128)}, u32[]{:S(2)}) copy-start(f32[128,512]{1,0:T(8,128)} %copy-done.19) | copy-start | bytes 786436
  1406.0 242.6 %all-to-all-start.2 = ((f32[8,16,512]{2,1,0:T(8,128)}), f32[8,16,512]{2,1,0:T(8,128)S(1)}, u32[]{:S(2)}, u32[]{:S(2)}) async-start(f32[8,16,512]{2,1,0:T(8,128)} %bitcast.87), calls=%async_computation.2 | async-start | bytes 524288 | tf_op jit(solution)/shard_map/all_to_all | solution.py:161
  (9 other events, 32.4 us)
Sparse Core Ops, SparseCore 0:
  49.7 248.4 all-reduce.18
  325.0 65.4 all-reduce.30
  394.0 146.5 all-reduce.26
  732.9 239.8 all-reduce.20
  993.4 68.8 all-reduce.28
  1065.6 146.5 all-reduce.24
  1406.1 239.8 all-reduce.22
